TPU v7x, 512 devices: a whole 4x8x8 slice. The times are simulated.
512 devices in a mesh: tm: 128 (over y, z, x_lo), batch: 4 (over x_hi, core).
Axes of the slice: x: 4 (x_hi: 2, x_lo: 2; x = x_hi * 2 + x_lo), y: 8, z: 8, core: 2. Of those that a mesh axis runs over, the one named last changes fastest.
Arguments:
- signal: bfloat16 [16, 16384, 64], P('batch', 'tm'), may hold values from -6 to 6
- skip_grad: bfloat16 [16, 16384, 128], P('batch', 'tm'), may hold values from -24 to 24
- stream_grad: bfloat16 [16, 16384, 64], P('batch', 'tm'), may hold values from -24 to 24
- w_past: bfloat16 [5, 64, 512], replicated, may hold values from -0.5 to 0.5
- w_now: bfloat16 [5, 64, 512], replicated, may hold values from -0.5 to 0.5
- w_res: bfloat16 [5, 256, 64], replicated, may hold values from -0.375 to 0.375
- w_skip: bfloat16 [5, 256, 128], replicated, may hold values from -0.375 to 0.375
Outputs:
- skip_out: bfloat16 [16, 16384, 128], P('batch', 'tm')
- stream_out: bfloat16 [16, 16384, 64], P('batch', 'tm')
- signal_cot: bfloat16 [16, 16384, 64], P('batch', 'tm')
- g_past: bfloat16 [5, 64, 512], replicated
- g_now: bfloat16 [5, 64, 512], replicated
- g_res: bfloat16 [5, 256, 64], replicated
- g_skip: bfloat16 [5, 256, 128], replicated
All inputs are finite; a program needn't handle non-finite values.
Results may differ from a plain program's by a relative error of at most 0.015.
Values may be sent and summed in bfloat16 or wider, within the bound.
A program may use at most 64 MiB of HBM per device.

v0:
```python
import math
import jax
import jax.numpy as jnp
from jax import lax
from jax.sharding import PartitionSpec as P


def from_behind(block, axis, distance):
    devices = range(lax.axis_size(axis))
    route = [(i - distance, i) for i in devices if i - distance in devices]
    return lax.ppermute(block, axis, route)


def product(left, right):
    return jnp.einsum("str,rc->stc", left, right, preferred_element_type=jnp.float32)


def product_transposed(left, right):
    return jnp.einsum("stc,rc->str", left, right, preferred_element_type=jnp.float32)


def column_sum(left, right):
    return jnp.einsum("str,stc->rc", left, right, preferred_element_type=jnp.float32)


def forward_layer(stream, delayed, layer, w_past, w_now, w_res, w_skip, records, skip_acc):
    gate_width = w_res.shape[1]
    preact = product(delayed, w_past[layer]) + product(stream, w_now[layer])
    gated = (
        jnp.tanh(preact[:, :, :gate_width]) * jax.nn.sigmoid(preact[:, :, gate_width:])
    ).astype(jnp.bfloat16)
    records.append((delayed, stream, preact, gated))
    skip_acc = skip_acc + product(gated, w_skip[layer])
    stream = (stream.astype(jnp.float32) + product(gated, w_res[layer])).astype(jnp.bfloat16)
    return (stream, skip_acc)


def on_device(signal, skip_grad, stream_grad, w_past, w_now, w_res, w_skip):
    stream = signal
    seq_count = stream.shape[0]
    rows = stream.shape[1]
    base_step = rows // 16
    layers = w_past.shape[0]
    gate_width = w_res.shape[1]
    near_layers = 4
    records = []
    skip_acc = jnp.zeros((seq_count, rows, w_skip.shape[2]), jnp.float32)
    for layer in range(near_layers):
        dilation = base_step * 2**layer
        edge_rows = from_behind(stream[:, rows - dilation :], "tm", 1)
        delayed = jnp.concatenate([edge_rows, stream[:, : rows - dilation]], 1)
        stream, skip_acc = forward_layer(
            stream, delayed, layer, w_past, w_now, w_res, w_skip, records, skip_acc
        )
    layer = 4
    hops = base_step * 2**layer // rows
    delayed = from_behind(stream, "tm", hops)
    stream, skip_acc = forward_layer(
        stream, delayed, layer, w_past, w_now, w_res, w_skip, records, skip_acc
    )
    skip_out = skip_acc.astype(jnp.bfloat16)
    flow = stream_grad.astype(jnp.float32)
    grads = [None] * layers
    for layer in reversed(range(layers)):
        dilation = base_step * 2**layer
        delayed, current, preact, gated = records[layer]
        filt = jnp.tanh(preact[:, :, :gate_width])
        sigm = jax.nn.sigmoid(preact[:, :, gate_width:])
        flow_half = flow.astype(jnp.bfloat16)
        gated_cot = product_transposed(skip_grad, w_skip[layer]) + product_transposed(
            flow_half, w_res[layer]
        )
        pre_cot = jnp.concatenate(
            [gated_cot * sigm * (1.0 - filt * filt), gated_cot * filt * sigm * (1.0 - sigm)], 2
        ).astype(jnp.bfloat16)
        local_grads = (
            column_sum(delayed, pre_cot),
            column_sum(current, pre_cot),
            column_sum(gated, flow_half),
            column_sum(gated, skip_grad),
        )
        grads[layer] = local_grads
        past_cot = product_transposed(pre_cot, w_past[layer]).astype(jnp.bfloat16)
        if dilation < rows:
            head_rows = from_behind(past_cot[:, :dilation], "tm", -1)
            moved = jnp.concatenate([past_cot[:, dilation:], head_rows], 1)
        else:
            moved = from_behind(past_cot, "tm", -(dilation // rows))
        flow = flow + product_transposed(pre_cot, w_now[layer]) + moved.astype(jnp.float32)
    signal_cot = flow.astype(jnp.bfloat16)
    stacked = tuple(
        (jnp.stack([grads[layer][which] for layer in range(layers)]) for which in range(4))
    )
    scale = 1.0 / math.sqrt(seq_count * lax.axis_size("batch") * rows * lax.axis_size("tm"))
    totals = lax.psum(stacked, ("tm", "batch"))
    finals = tuple(((total * scale).astype(jnp.bfloat16) for total in totals))
    return (skip_out, stream, signal_cot, finals[0], finals[1], finals[2], finals[3])


def solution(mesh):
    placed = (
        P("batch", "tm", None),
        P("batch", "tm", None),
        P("batch", "tm", None),
        P(),
        P(),
        P(),
        P(),
    )
    return jax.shard_map(
        on_device,
        mesh=mesh,
        in_specs=placed,
        out_specs=(
            P("batch", "tm", None),
            P("batch", "tm", None),
            P("batch", "tm", None),
            P(),
            P(),
            P(),
            P(),
        ),
        check_vma=False,
    )
```

profile of v0, /device:TPU:17, one launch (start us, length us, event | category | flops | bytes accessed | tf_op | source)
XLA Modules:
  0.0 407.3 jit_solution(14410823166842004948)
XLA Ops:
  7.2 1.0 slice.168
  8.2 3.3 collective-permute-start
  11.5 1.1 fusion.46
  13.3 0.6 copy-done.2
  14.6 6.9 %collective-permute-done = bf16[4,8,64]{1,2,0:T(8,128)(2,1)S(1)} collective-permute-done((bf16[4,8,64]{1,2,0:T(8,128)(2,1)S(1)}, bf16[4,8,64]{1,2,0:T(8,128)(2,1)S(1)}, u32[]{:S(2)}, u32[]{:S(2)}) %collective-permute-start) | collective-permute-done | bytes 4128 | tf_op jit(solution)/shard_map/ppermute | solution.py:11
  22.3 0.7 copy-done.11
  23.6 1.9 collective-permute-start.1
  25.8 5.8 %collective-permute-done.1 = bf16[4,16,64]{1,2,0:T(8,128)(2,1)S(1)} collective-permute-done((bf16[4,16,64]{1,2,0:T(8,128)(2,1)S(1)}, bf16[4,16,64]{1,2,0:T(8,128)(2,1)S(1)}, u32[]{:S(2)}, u32[]{:S(2)}) %collective-permute-start.1) | collective-permute-done | bytes 8224 | tf_op jit(solution)/shard_map/ppermute | solution.py:11
  33.1 1.9 collective-permute-start.2
  35.3 5.8 %collective-permute-done.2 = bf16[4,32,64]{1,2,0:T(8,128)(2,1)S(1)} collective-permute-done((bf16[4,32,64]{1,2,0:T(8,128)(2,1)S(1)}, bf16[4,32,64]{1,2,0:T(8,128)(2,1)S(1)}, u32[]{:S(2)}, u32[]{:S(2)}) %collective-permute-start.2) | collective-permute-done | bytes 16416 | tf_op jit(solution)/shard_map/ppermute | solution.py:11
  42.1 1.9 collective-permute-start.3
  44.3 5.8 %collective-permute-done.3 = bf16[4,64,64]{1,2,0:T(8,128)(2,1)S(1)} collective-permute-done((bf16[4,64,64]{1,2,0:T(8,128)(2,1)S(1)}, bf16[4,64,64]{1,2,0:T(8,128)(2,1)S(1)}, u32[]{:S(2)}, u32[]{:S(2)}) %collective-permute-start.3) | collective-permute-done | bytes 32800 | tf_op jit(solution)/shard_map/ppermute | solution.py:11
  50.9 1.9 collective-permute-start.4
  53.2 5.8 %collective-permute-done.4 = bf16[4,128,64]{1,2,0:T(8,128)(2,1)S(1)} collective-permute-done((bf16[4,128,64]{1,2,0:T(8,128)(2,1)S(1)}, bf16[4,128,64]{1,2,0:T(8,128)(2,1)S(1)}, u32[]{:S(2)}, u32[]{:S(2)}) %collective-permute-start.4) | collective-permute-done | bytes 65568 | tf_op jit(solution)/shard_map/ppermute | solution.py:11
  60.0 1.9 collective-permute-start.5
  62.2 2.9 collective-permute-done.5
  66.2 4.8 %collective-permute-start.6 = (bf16[4,64,64]{1,2,0:T(8,128)(2,1)S(1)}, bf16[4,64,64]{1,2,0:T(8,128)(2,1)S(1)}, u32[]{:S(2)}, u32[]{:S(2)}) collective-permute-start(bf16[4,64,64]{1,2,0:T(8,128)(2,1)S(1)} %get-tuple-element.23), channel_id=1, source_target_pairs={{4,0},{8,4},{12,8},{16,12},{20,16},{24,20},{28,24},{32,28},{36,32}... | collective-permute-start | bytes 98312 | tf_op jit(solution)/shard_map/ppermute | solution.py:11
  71.3 1.0 collective-permute-done.6
  73.4 6.7 %collective-permute-start.7 = (bf16[4,32,64]{1,2,0:T(8,128)(2,1)S(1)}, bf16[4,32,64]{1,2,0:T(8,128)(2,1)S(1)}, u32[]{:S(2)}, u32[]{:S(2)}) collective-permute-start(bf16[4,32,64]{1,2,0:T(8,128)(2,1)S(1)} %bitcast.291), channel_id=1, source_target_pairs={{4,0},{8,4},{12,8},{16,12},{20,16},{24,20},{28,24},{32,28},{36,32}... | collective-permute-start | bytes 49160 | tf_op jit(solution)/shard_map/ppermute | solution.py:11
  80.4 0.9 collective-permute-done.7
  82.4 6.7 %collective-permute-start.8 = (bf16[4,16,64]{1,2,0:T(8,128)(2,1)S(1)}, bf16[4,16,64]{1,2,0:T(8,128)(2,1)S(1)}, u32[]{:S(2)}, u32[]{:S(2)}) collective-permute-start(bf16[4,16,64]{1,2,0:T(8,128)(2,1)S(1)} %bitcast.289), channel_id=1, source_target_pairs={{4,0},{8,4},{12,8},{16,12},{20,16},{24,20},{28,24},{32,28},{36,32}... | collective-permute-start | bytes 24584 | tf_op jit(solution)/shard_map/ppermute | solution.py:11
  89.5 1.1 collective-permute-done.8
  91.1 0.5 copy-done.12
  95.8 0.8 copy-done.6
  96.9 0.9 fusion
  98.2 6.8 %collective-permute-start.9 = (bf16[4,8,64]{1,2,0:T(8,128)(2,1)S(1)}, bf16[4,8,64]{1,2,0:T(8,128)(2,1)S(1)}, u32[]{:S(2)}, u32[]{:S(2)}) collective-permute-start(bf16[4,8,64]{1,2,0:T(8,128)(2,1)S(1)} %bitcast.290), channel_id=1, source_target_pairs={{4,0},{8,4},{12,8},{16,12},{20,16},{24,20},{28,24},{32,28},{36,32}... | collective-permute-start | bytes 12296 | tf_op jit(solution)/shard_map/ppermute | solution.py:11
  105.0 0.8 fusion.24
  106.8 1.8 fusion.25
  108.5 287.3 %all-reduce.3.cloned.1.call-done = (f32[5,64,512]{2,1,0:T(8,128)}, f32[5,64,512]{2,1,0:T(8,128)}, f32[5,256,64]{1,2,0:T(8,128)}, f32[5,256,128]{2,1,0:T(8,128)}) async-done(((f32[5,64,512]{2,1,0:T(8,128)}, f32[5,64,512]{2,1,0:T(8,128)}, f32[5,256,64]{1,2,0:T(8,128)}, f32[5,256,128]{2,1,0:T(8,128)}), (f32[5,64,512]{2,1,0:T(8,128)}, f32[5,64,512]{2,1,0:T(8,128)}, f32[5,256,64]{1,2,0:T(8,128)}, ...) | async-done | bytes 2293776 | tf_op jit(solution)/shard_map/psum | solution.py:95
  395.8 1.8 multiply_convert_fusion.18
  397.6 1.9 multiply_convert_fusion
  399.4 1.0 multiply_convert_fusion.1
  (104 shorter events, 18.7 us)
Async XLA Ops:
  7.2 4.3 %copy-start = (bf16[4,128,128]{2,1,0:T(8,128)(2,1)S(1)}, bf16[4,128,128]{2,1,0:T(8,128)(2,1)}, u32[]{:S(2)}) copy-start(bf16[4,128,128]{2,1,0:T(8,128)(2,1)} %param.8) | copy-start | bytes 393220
  7.2 388.6 %all-reduce.3.cloned.1.call-start = ((), (), s32[]{:S(2)}) async-start(), calls=%async_computation | async-start | bytes 4587520 | tf_op jit(solution)/shard_map/psum | solution.py:95
  8.2 4.4 %copy-start.1 = (bf16[5,256,128]{2,1,0:T(8,128)(2,1)S(1)}, bf16[5,256,128]{2,1,0:T(8,128)(2,1)}, u32[]{:S(2)}) copy-start(bf16[5,256,128]{2,1,0:T(8,128)(2,1)} %param.13) | copy-start | bytes 983044
  8.2 13.3 %collective-permute-start = (bf16[4,8,64]{1,2,0:T(8,128)(2,1)S(1)}, bf16[4,8,64]{1,2,0:T(8,128)(2,1)S(1)}, u32[]{:S(2)}, u32[]{:S(2)}) collective-permute-start(bf16[4,8,64]{1,2,0:T(8,128)(2,1)S(1)} %slice.168), channel_id=1, source_target_pairs={{0,4},{4,8},{8,12},{12,16},{16,20},{20,24},{24,28},{28,32},{32,36}... | collective-permute-start | bytes 12296 | tf_op jit(solution)/shard_map/ppermute | solution.py:11
  13.0 0.8 copy-start.2
  13.0 1.0 copy-start.10
  14.3 7.1 %copy-start.9 = (bf16[5,64,512]{2,1,0:T(8,128)(2,1)S(1)}, bf16[5,64,512]{2,1,0:T(8,128)(2,1)}, u32[]{:S(2)}) copy-start(bf16[5,64,512]{2,1,0:T(8,128)(2,1)} %param.10) | copy-start | bytes 983044
  22.1 0.9 copy-start.11
  23.6 8.0 %collective-permute-start.1 = (bf16[4,16,64]{1,2,0:T(8,128)(2,1)S(1)}, bf16[4,16,64]{1,2,0:T(8,128)(2,1)S(1)}, u32[]{:S(2)}, u32[]{:S(2)}) collective-permute-start(bf16[4,16,64]{1,2,0:T(8,128)(2,1)S(1)} %slice.216), channel_id=1, source_target_pairs={{0,4},{4,8},{8,12},{12,16},{16,20},{20,24},{24,28},{28,32},{32,36}... | collective-permute-start | bytes 24584 | tf_op jit(solution)/shard_map/ppermute | solution.py:11
  33.1 8.0 %collective-permute-start.2 = (bf16[4,32,64]{1,2,0:T(8,128)(2,1)S(1)}, bf16[4,32,64]{1,2,0:T(8,128)(2,1)S(1)}, u32[]{:S(2)}, u32[]{:S(2)}) collective-permute-start(bf16[4,32,64]{1,2,0:T(8,128)(2,1)S(1)} %slice.220), channel_id=1, source_target_pairs={{0,4},{4,8},{8,12},{12,16},{16,20},{20,24},{24,28},{28,32},{32,36}... | collective-permute-start | bytes 49160 | tf_op jit(solution)/shard_map/ppermute | solution.py:11
  42.1 8.0 %collective-permute-start.3 = (bf16[4,64,64]{1,2,0:T(8,128)(2,1)S(1)}, bf16[4,64,64]{1,2,0:T(8,128)(2,1)S(1)}, u32[]{:S(2)}, u32[]{:S(2)}) collective-permute-start(bf16[4,64,64]{1,2,0:T(8,128)(2,1)S(1)} %get-tuple-element.24), channel_id=1, source_target_pairs={{0,4},{4,8},{8,12},{12,16},{16,20},{20,24},{24,28},{28,32},{32,36}... | collective-permute-start | bytes 98312 | tf_op jit(solution)/shard_map/ppermute | solution.py:11
  50.9 8.0 %collective-permute-start.4 = (bf16[4,128,64]{1,2,0:T(8,128)(2,1)S(1)}, bf16[4,128,64]{1,2,0:T(8,128)(2,1)S(1)}, u32[]{:S(2)}, u32[]{:S(2)}) collective-permute-start(bf16[4,128,64]{1,2,0:T(8,128)(2,1)S(1)} %fusion.23), channel_id=1, source_target_pairs={{0,4},{4,8},{8,12},{12,16},{16,20},{20,24},{24,28},{28,32},{32,36}... | collective-permute-start | bytes 196616 | tf_op jit(solution)/shard_map/ppermute | solution.py:11
  53.2 6.1 %copy-start.14 = (bf16[4,128,64]{1,2,0:T(8,128)(2,1)S(1)}, bf16[4,128,64]{1,2,0:T(8,128)(2,1)}, u32[]{:S(2)}) copy-start(bf16[4,128,64]{1,2,0:T(8,128)(2,1)} %param.9) | copy-start | bytes 196612
  60.0 5.1 %collective-permute-start.5 = (bf16[4,128,64]{1,2,0:T(8,128)(2,1)S(1)}, bf16[4,128,64]{1,2,0:T(8,128)(2,1)S(1)}, u32[]{:S(2)}, u32[]{:S(2)}) collective-permute-start(bf16[4,128,64]{1,2,0:T(8,128)(2,1)S(1)} %convolution_convert_fusion.4), channel_id=1, source_target_pairs={{4,0},{8,4},{12,8},{16,12},{20,16},{24,20},{28,24},{32,28},{36,32}... | collective-permute-start | bytes 196616 | tf_op jit(solution)/shard_map/ppermute | solution.py:11
  66.2 6.2 %collective-permute-start.6 = (bf16[4,64,64]{1,2,0:T(8,128)(2,1)S(1)}, bf16[4,64,64]{1,2,0:T(8,128)(2,1)S(1)}, u32[]{:S(2)}, u32[]{:S(2)}) collective-permute-start(bf16[4,64,64]{1,2,0:T(8,128)(2,1)S(1)} %get-tuple-element.23), channel_id=1, source_target_pairs={{4,0},{8,4},{12,8},{16,12},{20,16},{24,20},{28,24},{32,28},{36,32}... | collective-permute-start | bytes 98312 | tf_op jit(solution)/shard_map/ppermute | solution.py:11
  73.4 8.0 %collective-permute-start.7 = (bf16[4,32,64]{1,2,0:T(8,128)(2,1)S(1)}, bf16[4,32,64]{1,2,0:T(8,128)(2,1)S(1)}, u32[]{:S(2)}, u32[]{:S(2)}) collective-permute-start(bf16[4,32,64]{1,2,0:T(8,128)(2,1)S(1)} %bitcast.291), channel_id=1, source_target_pairs={{4,0},{8,4},{12,8},{16,12},{20,16},{24,20},{28,24},{32,28},{36,32}... | collective-permute-start | bytes 49160 | tf_op jit(solution)/shard_map/ppermute | solution.py:11
  82.4 8.2 %collective-permute-start.8 = (bf16[4,16,64]{1,2,0:T(8,128)(2,1)S(1)}, bf16[4,16,64]{1,2,0:T(8,128)(2,1)S(1)}, u32[]{:S(2)}, u32[]{:S(2)}) collective-permute-start(bf16[4,16,64]{1,2,0:T(8,128)(2,1)S(1)} %bitcast.289), channel_id=1, source_target_pairs={{4,0},{8,4},{12,8},{16,12},{20,16},{24,20},{28,24},{32,28},{36,32}... | collective-permute-start | bytes 24584 | tf_op jit(solution)/shard_map/ppermute | solution.py:11
  89.4 1.7 copy-start.3
  90.9 0.7 copy-start.12
  92.0 2.1 copy-start.15
  92.0 2.1 copy-start.17
  93.1 0.8 copy-start.7
  94.1 0.7 copy-start.8
  95.8 0.8 copy-start.6
  96.9 1.0 copy-start.16
  96.9 1.0 copy-start.18
  98.2 8.1 %collective-permute-start.9 = (bf16[4,8,64]{1,2,0:T(8,128)(2,1)S(1)}, bf16[4,8,64]{1,2,0:T(8,128)(2,1)S(1)}, u32[]{:S(2)}, u32[]{:S(2)}) collective-permute-start(bf16[4,8,64]{1,2,0:T(8,128)(2,1)S(1)} %bitcast.290), channel_id=1, source_target_pairs={{4,0},{8,4},{12,8},{16,12},{20,16},{24,20},{28,24},{32,28},{36,32}... | collective-permute-start | bytes 12296 | tf_op jit(solution)/shard_map/ppermute | solution.py:11
  105.9 0.9 copy-start.13
  395.8 3.6 copy-start.4
  395.8 3.6 copy-start.5
Sparse Core Ops, SparseCore 0:
  96.8 298.9 all-reduce.2
where the time goes:
time: 408 us; the launch traced here: 407 us
  waiting for transfers between devices  324 us (79%)
  starting transfers between devices  38 us (9%)
  matrix products  19.7 us (5%)
  between operations  14.6 us (4%)
  local copies, waits for them, and re-layouts  5.72 us (1%)
  other arithmetic  5.5 us (1%)
    psum x1, waiting for transfers between devices, on_device(): totals = lax.psum(stacked, ('tm', 'batch'))  287 us
    ppermute x10, starting transfers between devices, from_behind(): return lax.ppermute(block, axis, route)  37.9 us
    ppermute x10, waiting for transfers between devices, from_behind(): return lax.ppermute(block, axis, route)  36.5 us
    dot_general x20, matrix products, product_transposed(): jnp.einsum('stc,rc->str', left, right, preferred_element_type=jnp.float32)  8.4 us
  transfers between devices with their start and end apart: 11, of which 11 were waited for; matrix products, arithmetic and copies ran while one was open for 2% of the time, Pallas kernels for 0%

commit v1 on v0

--- a/solution.py
+++ b/solution.py
@@ -92,7 +92,7 @@
         (jnp.stack([grads[layer][which] for layer in range(layers)]) for which in range(4))
     )
     scale = 1.0 / math.sqrt(seq_count * lax.axis_size("batch") * rows * lax.axis_size("tm"))
-    totals = lax.psum(stacked, ("tm", "batch"))
+    totals = lax.psum(lax.psum(stacked, "tm"), "batch")
     finals = tuple(((total * scale).astype(jnp.bfloat16) for total in totals))
     return (skip_out, stream, signal_cot, finals[0], finals[1], finals[2], finals[3])
 

time: 408 us -> 1350 us (3.31)
  the two profiles are of different devices: /device:TPU:17 before, /device:TPU:1 now
where the time goes in v1:
time: 1350 us
  waiting for transfers between devices  1280 us (95%)
  starting transfers between devices  26.9 us (2%)
  matrix products  21.3 us (2%)
  between operations  14.6 us (1%)
    psum x2, waiting for transfers between devices, on_device(): totals = lax.psum(lax.psum(stacked, 'tm'), 'batch')  1250 us
  transfers between devices with their start and end apart: 12, of which 11 were waited for; matrix products, arithmetic and copies ran while one was open for 1% of the time, Pallas kernels for 0%

profile of v1, /device:TPU:1, one launch (start us, length us, event | category | flops | bytes accessed | tf_op | source)
XLA Modules:
  0.0 1351.7 jit_solution(10419703297262068471)
XLA Ops:
  7.2 1.0 slice.168
  8.2 4.1 collective-permute-start
  12.3 1.1 fusion.46
  15.4 0.7 copy-done.9
  18.1 4.0 collective-permute-start.1
  22.3 1.0 collective-permute-done.1
  24.3 3.7 collective-permute-start.2
  28.3 1.0 collective-permute-done.2
  30.2 4.0 collective-permute-start.3
  34.6 1.0 collective-permute-done.3
  36.4 4.6 collective-permute-start.4
  41.3 1.0 collective-permute-done.4
  43.4 1.3 collective-permute-start.5
  45.0 4.7 collective-permute-done.5
  50.7 1.3 collective-permute-start.6
  52.3 4.7 collective-permute-done.6
  58.0 1.3 collective-permute-start.7
  59.6 4.7 collective-permute-done.7
  65.3 1.3 collective-permute-start.8
  67.0 5.3 collective-permute-done.8
  77.4 0.8 copy-done.6
  78.3 1118.1 %all-reduce.5.cloned.1.call-done = (f32[5,64,512]{2,1,0:T(8,128)}, f32[5,64,512]{2,1,0:T(8,128)}, f32[5,256,64]{1,2,0:T(8,128)}, f32[5,256,128]{2,1,0:T(8,128)}) async-done(((f32[5,64,512]{2,1,0:T(8,128)}, f32[5,64,512]{2,1,0:T(8,128)}, f32[5,256,64]{1,2,0:T(8,128)}, f32[5,256,128]{2,1,0:T(8,128)}), (f32[5,64,512]{2,1,0:T(8,128)}, f32[5,64,512]{2,1,0:T(8,128)}, f32[5,256,64]{1,2,0:T(8,128)}, ...) | async-done | bytes 2293776 | tf_op jit(solution)/shard_map/psum | solution.py:95
  1197.4 0.9 fusion
  1198.4 1.1 convolution_convert_fusion
  1199.5 1.3 collective-permute-start.9
  1200.8 1.6 fusion.24
  1202.5 2.5 collective-permute-done.9
  1205.0 1.8 fusion.25
  1206.8 133.5 %all-reduce.7.cloned.1.call-done = (f32[5,64,512]{2,1,0:T(8,128)}, f32[5,64,512]{2,1,0:T(8,128)}, f32[5,256,64]{1,2,0:T(8,128)}, f32[5,256,128]{2,1,0:T(8,128)}) async-done(((f32[5,64,512]{2,1,0:T(8,128)}, f32[5,64,512]{2,1,0:T(8,128)}, f32[5,256,64]{1,2,0:T(8,128)}, f32[5,256,128]{2,1,0:T(8,128)}), (f32[5,64,512]{2,1,0:T(8,128)}, f32[5,64,512]{2,1,0:T(8,128)}, f32[5,256,64]{1,2,0:T(8,128)}, ...) | async-done | bytes 2293776 | tf_op jit(solution)/shard_map/psum | solution.py:95
  1340.3 1.8 multiply_convert_fusion.18
  1342.0 1.9 multiply_convert_fusion
  1343.9 1.0 multiply_convert_fusion.1
  (107 shorter events, 19.4 us)
Async XLA Ops:
  7.2 5.1 copy-start
  7.2 1189.3 %all-reduce.5.cloned.1.call-start = ((), (), s32[]{:S(2)}) async-start(), calls=%async_computation | async-start | bytes 4587520 | tf_op jit(solution)/shard_map/psum | solution.py:95
  8.2 5.2 copy-start.1
  8.2 7.2 collective-permute-start
  13.8 0.8 copy-start.2
  13.8 1.0 copy-start.10
  15.2 1.0 copy-start.9
  16.5 0.9 copy-start.11
  18.1 5.3 collective-permute-start.1
  24.3 5.0 collective-permute-start.2
  30.2 5.3 collective-permute-start.3
  36.4 5.9 collective-permute-start.4
  41.3 1.3 copy-start.14
  43.4 6.2 collective-permute-start.5
  50.7 6.2 collective-permute-start.6
  58.0 6.3 collective-permute-start.7
  65.3 6.9 collective-permute-start.8
  66.9 5.8 copy-start.3
  72.5 0.7 copy-start.12
  73.6 2.1 copy-start.15
  73.6 2.1 copy-start.17
  74.7 0.8 copy-start.7
  75.7 0.7 copy-start.8
  77.4 0.8 copy-start.6
  78.3 1262.0 %all-reduce.7.cloned.1.call-start = ((), (), s32[]{:S(2)}) async-start(), calls=%async_computation.1 | async-start | bytes 4587520 | tf_op jit(solution)/shard_map/psum | solution.py:95
  1197.4 1.0 copy-start.16
  1197.4 1.0 copy-start.18
  1199.5 5.5 collective-permute-start.9
  1202.4 2.6 copy-start.13
  1340.3 3.6 copy-start.4
  1340.3 3.6 copy-start.5
Sparse Core Ops, SparseCore 0:
  78.4 1118.0 all-reduce.4
  1200.0 140.2 all-reduce.6
